TPU v7x, 128 devices: a whole 4x4x4 slice. The times are simulated.
128 devices in a mesh: dp: 4 (over z_hi, core), blk: 8 (over z_lo, y), ulysses: 4 (over x).
Axes of the slice: x: 4, y: 4, z: 4 (z_hi: 2, z_lo: 2; z = z_hi * 2 + z_lo), core: 2. Of those that a mesh axis runs over, the one named last changes fastest.
Arguments:
- queries: bfloat16 [4, 4096, 2048], P('dp', ('blk', 'ulysses')), may hold values from -8 to 8
- key_vectors: bfloat16 [4, 4096, 512], P('dp', ('blk', 'ulysses')), may hold values from -6 to 6
- value_vectors: bfloat16 [4, 4096, 512], P('dp', ('blk', 'ulysses')), may hold values from -6 to 6
- positions: int32 [4, 4096], P('dp'), may hold values from 0 to 4095, as said below
- out_weight: bfloat16 [2048, 4096], P(('dp', 'blk'), 'ulysses'), may hold values from -0.125 to 0.125
- out_grad: bfloat16 [4, 4096, 4096], P('dp', 'blk', 'ulysses'), may hold values from -6 to 6
Outputs:
- layer_output: bfloat16 [4, 4096, 4096], P('dp', 'blk', 'ulysses')
- query_grad: bfloat16 [4, 4096, 2048], P('dp', ('blk', 'ulysses'))
- key_grad: bfloat16 [4, 4096, 512], P('dp', ('blk', 'ulysses'))
- value_grad: bfloat16 [4, 4096, 512], P('dp', ('blk', 'ulysses'))
- weight_grad: float32 [2048, 4096], P(('dp', 'blk'), 'ulysses')
Inputs may be any that keep to these rules, and one draw needn't show every extreme that they name: Every position of a sequence appears once. Tokens come in runs of 256 that hold consecutive positions, each run starting at a multiple of 256; the tokens of one index of blk are two such runs.
All inputs are finite; a program needn't handle non-finite values.
Results may differ from a plain program's by a relative error of at most 0.035.
Values may be sent and summed in bfloat16 or wider, within the bound.
No kernel may reach another device: no remote copies, remote signals or barrier semaphores. Data moves between devices by JAX's collectives and lax.ppermute only.
A program may use at most 192 MiB of HBM per device.

v0:
```python
import jax
import jax.numpy as jnp
from jax import lax
from jax.sharding import PartitionSpec as P

HD = 128


MASKED_SCORE = -1e30


def from_behind(array, axis, by):
    length = lax.axis_size(axis)
    return lax.ppermute(array, axis, [(i, (i + by) % length) for i in range(length)])


def block_length():
    return 512


def score_tile(query_groups, key_block, query_place, key_place, softmax_scale):
    scores = (
        jnp.einsum("qcgd,kcd->qcgk", query_groups, key_block, preferred_element_type=jnp.float32)
        * softmax_scale
    )
    visible = key_place[None, None, None, :] <= query_place[:, None, None, None]
    return (scores, visible)


def forward_tile(
    state_now, query_groups, key_block, value_block, query_place, key_place, softmax_scale
):
    running_max, row_total, weighted = state_now
    scores, visible = score_tile(query_groups, key_block, query_place, key_place, softmax_scale)
    peak = jnp.max(jnp.where(visible, scores, MASKED_SCORE), axis=3)
    fresh_max = jnp.maximum(running_max, peak)
    factor = jnp.exp(running_max - fresh_max)
    weights = jnp.where(visible, jnp.exp(scores - fresh_max[..., None]), 0.0)
    row_total = row_total * factor + jnp.sum(weights, axis=3)
    weighted = weighted * factor[..., None] + jnp.einsum(
        "qcgk,kcd->qcgd",
        weights.astype(jnp.bfloat16),
        value_block,
        preferred_element_type=jnp.float32,
    )
    return (fresh_max, row_total, weighted)


def attend_keys(
    state_now, query_groups, key_rows, value_rows, query_place, key_place, softmax_scale
):
    length = key_rows.shape[0]
    tile_keys = block_length()
    count_blocks = length // tile_keys
    key_split = key_rows.reshape(count_blocks, tile_keys, key_rows.shape[1], key_rows.shape[2])
    value_split = value_rows.reshape(
        count_blocks, tile_keys, value_rows.shape[1], value_rows.shape[2]
    )
    place_split = key_place.reshape(count_blocks, tile_keys)

    def attend_one_block(state_in, block_items):
        key_block, value_block, place_block = block_items
        state_out = forward_tile(
            state_in, query_groups, key_block, value_block, query_place, place_block, softmax_scale
        )
        return (state_out, None)

    state_now, ignored = lax.scan(
        attend_one_block, state_now, (key_split, value_split, place_split)
    )
    return state_now


def backward_tile(
    query_groups,
    grad_heads,
    key_block,
    value_block,
    query_place,
    key_place,
    log_total,
    dot_term,
    softmax_scale,
):
    scores, visible = score_tile(query_groups, key_block, query_place, key_place, softmax_scale)
    probs = jnp.where(visible, jnp.exp(scores - log_total[..., None]), 0.0)
    prob_grad = jnp.einsum(
        "cgdq,kcd->qcgk", grad_heads, value_block, preferred_element_type=jnp.float32
    )
    score_grad = (probs * (prob_grad - dot_term[..., None]) * softmax_scale).astype(jnp.bfloat16)
    query_part = jnp.einsum(
        "qcgk,kcd->qcgd", score_grad, key_block, preferred_element_type=jnp.float32
    )
    key_part = jnp.einsum(
        "qcgk,qcgd->kcd", score_grad, query_groups, preferred_element_type=jnp.float32
    )
    value_part = jnp.einsum(
        "qcgk,cgdq->kcd", probs.astype(jnp.bfloat16), grad_heads, preferred_element_type=jnp.float32
    )
    return (query_part, key_part, value_part)


def gradient_keys(
    query_groups,
    grad_heads,
    key_rows,
    value_rows,
    query_place,
    key_place,
    log_total,
    dot_term,
    softmax_scale,
):
    length = key_rows.shape[0]
    tile_keys = block_length()
    count_blocks = length // tile_keys
    kv_local = key_rows.shape[1]
    key_split = key_rows.reshape(count_blocks, tile_keys, kv_local, key_rows.shape[2])
    value_split = value_rows.reshape(count_blocks, tile_keys, kv_local, value_rows.shape[2])
    place_split = key_place.reshape(count_blocks, tile_keys)

    def gradient_one_block(query_sum, block_items):
        key_block, value_block, place_block = block_items
        parts_now = backward_tile(
            query_groups,
            grad_heads,
            key_block,
            value_block,
            query_place,
            place_block,
            log_total,
            dot_term,
            softmax_scale,
        )
        return (query_sum + parts_now[0], (parts_now[1], parts_now[2]))

    start_sum = jnp.zeros(query_groups.shape, jnp.float32)
    query_sum, (key_blocks, value_blocks) = lax.scan(
        gradient_one_block, start_sum, (key_split, value_split, place_split)
    )
    key_terms = key_blocks.reshape(length, kv_local, key_rows.shape[2])
    value_terms = value_blocks.reshape(length, kv_local, value_rows.shape[2])
    return (query_sum, key_terms, value_terms)


def shards(queries, key_vectors, value_vectors, positions, out_weight, out_grad):
    blocks = lax.axis_size("blk")
    cycle_index = lax.axis_index("blk")
    query_heads, key_heads, value_heads = (
        lax.all_to_all(queries, "ulysses", split_axis=2, concat_axis=1, tiled=True),
        lax.all_to_all(key_vectors, "ulysses", split_axis=2, concat_axis=1, tiled=True),
        lax.all_to_all(value_vectors, "ulysses", split_axis=2, concat_axis=1, tiled=True),
    )
    weight_whole = lax.all_gather(out_weight, ("dp", "blk"), axis=0, tiled=True)
    block_rows = query_heads.shape[1]
    kv_local = key_heads.shape[2] // HD
    group_size = query_heads.shape[2] // key_heads.shape[2]
    softmax_scale = HD ** (-0.5)
    query_groups = query_heads[0].reshape(block_rows, kv_local, group_size, HD)
    key_local = key_heads[0].reshape(block_rows, kv_local, HD)
    value_local = value_heads[0].reshape(block_rows, kv_local, HD)
    seq_place = positions[0]
    query_place = lax.dynamic_slice_in_dim(seq_place, cycle_index * block_rows, block_rows)
    start_state = (
        jnp.full((block_rows, kv_local, group_size), MASKED_SCORE, jnp.float32),
        jnp.zeros((block_rows, kv_local, group_size), jnp.float32),
        jnp.zeros((block_rows, kv_local, group_size, HD), jnp.float32),
    )
    key_piece = lax.all_gather(key_heads, "blk", axis=1, tiled=True)[0].reshape(-1, kv_local, HD)
    value_piece = lax.all_gather(value_heads, "blk", axis=1, tiled=True)[0].reshape(
        -1, kv_local, HD
    )
    running_max, row_total, weighted = attend_keys(
        start_state, query_groups, key_piece, value_piece, query_place, seq_place, softmax_scale
    )
    attention_heads = (weighted / row_total[..., None]).astype(jnp.bfloat16)
    log_total = running_max + jnp.log(row_total)
    attention_rows = attention_heads.reshape(block_rows, kv_local * group_size * HD)
    attention_full = lax.all_gather(attention_rows, "ulysses", axis=1, tiled=True)
    layer_output = jnp.dot(attention_full, weight_whole, preferred_element_type=jnp.float32).astype(
        jnp.bfloat16
    )
    grad_columns = out_grad[0]
    attention_grad = lax.psum_scatter(
        jnp.einsum("fc,tc->ft", weight_whole, grad_columns, preferred_element_type=jnp.float32),
        "ulysses",
        scatter_dimension=0,
        tiled=True,
    )
    attention_grad = attention_grad.astype(jnp.bfloat16)
    weight_grad = lax.psum_scatter(
        jnp.einsum("tf,tc->fc", attention_full, grad_columns, preferred_element_type=jnp.float32),
        ("dp", "blk"),
        scatter_dimension=0,
        tiled=True,
    )
    grad_heads = attention_grad.reshape(kv_local, group_size, HD, block_rows)
    dot_term = jnp.einsum(
        "cgdq,qcgd->qcg", grad_heads, attention_heads, preferred_element_type=jnp.float32
    )
    key_current = key_local
    value_current = value_local
    query_sum = jnp.zeros((block_rows, kv_local, group_size, HD), jnp.float32)
    key_total = jnp.zeros((block_rows, kv_local, HD), jnp.float32)
    value_total = jnp.zeros((block_rows, kv_local, HD), jnp.float32)
    for cycle_step in range(blocks):
        source = (cycle_index - cycle_step) % blocks
        key_place = lax.dynamic_slice_in_dim(seq_place, source * block_rows, block_rows)
        query_part, key_part, value_part = gradient_keys(
            query_groups,
            grad_heads,
            key_current,
            value_current,
            query_place,
            key_place,
            log_total,
            dot_term,
            softmax_scale,
        )
        query_sum = query_sum + query_part
        key_total = key_total + key_part
        value_total = value_total + value_part
        if cycle_step + 1 < blocks:
            key_current, value_current = from_behind((key_current, value_current), "blk", 1)
        key_total, value_total = from_behind((key_total, value_total), "blk", 1)
    query_grad = query_sum.astype(jnp.bfloat16).reshape(1, block_rows, kv_local * group_size * HD)
    key_grad = key_total.astype(jnp.bfloat16).reshape(1, block_rows, kv_local * HD)
    value_grad = value_total.astype(jnp.bfloat16).reshape(1, block_rows, kv_local * HD)
    query_grad, key_grad, value_grad = (
        lax.all_to_all(query_grad, "ulysses", split_axis=1, concat_axis=2, tiled=True),
        lax.all_to_all(key_grad, "ulysses", split_axis=1, concat_axis=2, tiled=True),
        lax.all_to_all(value_grad, "ulysses", split_axis=1, concat_axis=2, tiled=True),
    )
    return (layer_output[None], query_grad, key_grad, value_grad, weight_grad)


def solution(mesh):
    in_specs = (
        P("dp", ("blk", "ulysses"), None),
        P("dp", ("blk", "ulysses"), None),
        P("dp", ("blk", "ulysses"), None),
        P("dp", None),
        P(("dp", "blk"), "ulysses"),
        P("dp", "blk", "ulysses"),
    )
    out_specs = (
        P("dp", "blk", "ulysses"),
        P("dp", ("blk", "ulysses"), None),
        P("dp", ("blk", "ulysses"), None),
        P("dp", ("blk", "ulysses"), None),
        P(("dp", "blk"), "ulysses"),
    )
    return jax.shard_map(shards, mesh=mesh, in_specs=in_specs, out_specs=out_specs, check_vma=False)
```

profile of v0, /device:TPU:0, one launch (start us, length us, event | category | flops | bytes accessed | tf_op | source)
XLA Modules:
  0.0 550.6 jit_solution(546096914058688752)
XLA Ops:
  11.1 10.2 %all_to_all.105 = bf16[4,2,8192]{2,1,0:T(2,128)(2,1)S(1)} all-to-all(bf16[4,2,8192]{2,1,0:T(2,128)(2,1)S(1)} %reshape.824), channel_id=1, replica_groups=mesh['dp'=4,'blk'=8,'ulysses'=4] {'ulysses'}, dimensions={0} | all-to-all | bytes 262144 | tf_op jit(solution)/shard_map/all_to_all | solution.py:151
  24.9 8.4 %all_to_all.106 = bf16[4,2,8192]{2,1,0:T(2,128)(2,1)S(1)} all-to-all(bf16[4,2,8192]{2,1,0:T(2,128)(2,1)S(1)} %reshape.828), channel_id=1, replica_groups=mesh['dp'=4,'blk'=8,'ulysses'=4] {'ulysses'}, dimensions={0} | all-to-all | bytes 262144 | tf_op jit(solution)/shard_map/all_to_all | solution.py:152
  35.0 11.6 %reduce.9 = bf16[2048,128]{1,0:T(8,128)(2,1)S(1)} reduce(bf16[2048,1,128]{2,1,0:T(2,128)(2,1)S(1)} %bitcast.821, bf16[]{:T(256)} %broadcast.330), dimensions={1}, to_apply=%bitcast.754.reduce_sub_computation | reduce | bytes 1048578
  52.6 6.4 %all-to-all-done.1 = bf16[4,2,32768]{2,1,0:T(2,128)(2,1)S(1)} async-done(((bf16[4,2,32768]{2,1,0:T(2,128)(2,1)}), bf16[4,2,32768]{2,1,0:T(2,128)(2,1)S(1)}, u32[]{:S(2)}, u32[]{:S(2)}) %all-to-all-start.1) | async-done | bytes 524320 | tf_op jit(solution)/shard_map/all_to_all | solution.py:150
  60.0 38.6 %all-gather.11.cloned.1.call-done = bf16[2048,1024]{1,0:T(8,128)(2,1)} async-done(((bf16[64,1024]{1,0:T(8,128)(2,1)}), bf16[2048,1024]{1,0:T(8,128)(2,1)}) %all-gather.11.cloned.1.call-update) | async-done | bytes 4194320 | tf_op jit(solution)/shard_map/all_gather | solution.py:154
  98.6 6.6 %fusion.212 = f32[2048,512]{1,0:T(8,128)} fusion(bf16[2048,1024]{1,0:T(8,128)(2,1)} %all-gather.11.cloned.1.call-done, bf16[1,512,1024]{2,1,0:T(8,128)(2,1)S(1)} %copy-done), kind=kOutput, calls=%fused_computation.182 | convolution fusion | flops 2147483648 | bytes 9437184 | tf_op jit(solution)/shard_map/fc,tc->ft/dot_general | solution.py:185
  105.5 35.9 %all-gather.5.cloned.1.call-done = bf16[1,4096,128]{2,1,0:T(8,128)(2,1)} async-done(((bf16[1,512,128]{2,1,0:T(8,128)(2,1)}), bf16[1,4096,128]{2,1,0:T(8,128)(2,1)}) %all-gather.5.cloned.1.call-update) | async-done | bytes 1048592 | tf_op jit(solution)/shard_map/all_gather | solution.py:169
  141.4 40.2 %all-gather.7.cloned.1.call-done = bf16[1,4096,128]{2,1,0:T(8,128)(2,1)} async-done(((bf16[1,512,128]{2,1,0:T(8,128)(2,1)}), bf16[1,4096,128]{2,1,0:T(8,128)(2,1)}) %all-gather.7.cloned.1.call-update) | async-done | bytes 1048592 | tf_op jit(solution)/shard_map/all_gather | solution.py:170
  181.7 69.1 %while.3 = (s32[]{:T(128)}, f32[512,1,4]{0,2,1:T(4,128)S(1)}, f32[512,1,4]{0,2,1:T(4,128)S(1)}, f32[512,1,4,128]{0,3,2,1:T(8,128)S(1)}, s32[8,512]{1,0:T(8,128)S...) while((s32[]{:T(128)}, f32[512,1,4]{0,2,1:T(4,128)S(1)}, ...), condition=%wide.region_3.4_spmd.clone, body=%wide.region_0.3_spmd.clone.sunk | while | flops 549466112 | bytes 33432728 | solution.py:68
  181.9 3.8 fusion.306
  190.5 3.8 fusion.306
  199.1 3.8 fusion.306
  202.9 3.6 fusion.309
  207.8 3.8 fusion.306
  211.6 3.7 fusion.309
  216.4 3.8 fusion.306
  220.2 3.7 fusion.309
  225.1 3.8 fusion.306
  228.9 3.6 fusion.309
  233.8 3.8 fusion.306
  242.4 3.8 fusion.306
  253.1 29.8 %all-gather.9.cloned.1.call-done = bf16[512,2048]{0,1:T(8,128)(2,1)} async-done(((bf16[512,512]{0,1:T(8,128)(2,1)}), bf16[512,2048]{0,1:T(8,128)(2,1)}) %all-gather.9.cloned.1.call-update) | async-done | bytes 2097168 | tf_op jit(solution)/shard_map/all_gather | solution.py:179
  283.0 7.3 %fusion.210 = f32[2048,1024]{1,0:T(8,128)} fusion(bf16[512,2048]{0,1:T(8,128)(2,1)} %all-gather.9.cloned.1.call-done, bf16[1,512,1024]{2,1,0:T(8,128)(2,1)S(1)} %copy-done), kind=kOutput, calls=%fused_computation.180 | convolution fusion | flops 2147483648 | bytes 11534336 | tf_op jit(solution)/shard_map/tf,tc->fc/dot_general | solution.py:192
  294.1 5.5 %collective-permute-done = bf16[512,1,128]{2,0,1:T(8,128)(2,1)S(1)} collective-permute-done((bf16[512,1,128]{2,0,1:T(8,128)(2,1)S(1)}, bf16[512,1,128]{2,0,1:T(8,128)(2,1)S(1)}, u32[]{:S(2)}, u32[]{:S(2)}) %collective-permute-start) | collective-permute-done | bytes 131104 | tf_op jit(solution)/shard_map/ppermute | solution.py:14
  303.8 7.0 %collective-permute-done.2 = bf16[512,1,128]{2,0,1:T(8,128)(2,1)S(1)} collective-permute-done((bf16[512,1,128]{2,0,1:T(8,128)(2,1)S(1)}, bf16[512,1,128]{2,0,1:T(8,128)(2,1)S(1)}, u32[]{:S(2)}, u32[]{:S(2)}) %collective-permute-start.2) | collective-permute-done | bytes 131104 | tf_op jit(solution)/shard_map/ppermute | solution.py:14
  310.9 5.6 %collective-permute-done.3 = bf16[512,1,128]{2,0,1:T(8,128)(2,1)S(1)} collective-permute-done((bf16[512,1,128]{2,0,1:T(8,128)(2,1)S(1)}, bf16[512,1,128]{2,0,1:T(8,128)(2,1)S(1)}, u32[]{:S(2)}, u32[]{:S(2)}) %collective-permute-start.3) | collective-permute-done | bytes 131104 | tf_op jit(solution)/shard_map/ppermute | solution.py:14
  323.1 4.9 collective-permute-done.5
  328.0 5.8 %collective-permute-done.6 = bf16[512,1,128]{2,0,1:T(8,128)(2,1)S(1)} collective-permute-done((bf16[512,1,128]{2,0,1:T(8,128)(2,1)S(1)}, bf16[512,1,128]{2,0,1:T(8,128)(2,1)S(1)}, u32[]{:S(2)}, u32[]{:S(2)}) %collective-permute-start.6) | collective-permute-done | bytes 131104 | tf_op jit(solution)/shard_map/ppermute | solution.py:14
  334.9 4.5 collective-permute-done.7
  339.4 6.2 %collective-permute-done.8 = bf16[512,1,128]{2,0,1:T(8,128)(2,1)S(1)} collective-permute-done((bf16[512,1,128]{2,0,1:T(8,128)(2,1)S(1)}, bf16[512,1,128]{2,0,1:T(8,128)(2,1)S(1)}, u32[]{:S(2)}, u32[]{:S(2)}) %collective-permute-start.8) | collective-permute-done | bytes 131104 | tf_op jit(solution)/shard_map/ppermute | solution.py:14
  346.4 4.9 collective-permute-done.9
  351.3 5.8 %collective-permute-done.10 = bf16[512,1,128]{2,0,1:T(8,128)(2,1)S(1)} collective-permute-done((bf16[512,1,128]{2,0,1:T(8,128)(2,1)S(1)}, bf16[512,1,128]{2,0,1:T(8,128)(2,1)S(1)}, u32[]{:S(2)}, u32[]{:S(2)}) %collective-permute-start.10) | collective-permute-done | bytes 131104 | tf_op jit(solution)/shard_map/ppermute | solution.py:14
  357.9 4.9 collective-permute-done.11
  362.7 5.0 collective-permute-done.12
  396.6 4.8 reduce.11
  426.8 4.6 collective-permute-start.15
  431.4 8.6 %collective-permute-done.23 = f32[512,1,128]{0,2,1:T(8,128)S(1)} collective-permute-done((f32[512,1,128]{0,2,1:T(8,128)S(1)}, f32[512,1,128]{0,2,1:T(8,128)S(1)}, u32[]{:S(2)}, u32[]{:S(2)}) %collective-permute-start.23) | collective-permute-done | bytes 262176 | tf_op jit(solution)/shard_map/ppermute | solution.py:14
  442.6 8.6 %collective-permute-done.15 = f32[512,1,128]{2,0,1:T(8,128)S(1)} collective-permute-done((f32[512,1,128]{2,0,1:T(8,128)S(1)}, f32[512,1,128]{2,0,1:T(8,128)S(1)}, u32[]{:S(2)}, u32[]{:S(2)}) %collective-permute-start.15) | collective-permute-done | bytes 262176 | tf_op jit(solution)/shard_map/ppermute | solution.py:14
  453.1 8.0 %collective-permute-done.24 = f32[512,1,128]{0,2,1:T(8,128)S(1)} collective-permute-done((f32[512,1,128]{0,2,1:T(8,128)S(1)}, f32[512,1,128]{0,2,1:T(8,128)S(1)}, u32[]{:S(2)}, u32[]{:S(2)}) %collective-permute-start.24) | collective-permute-done | bytes 262176 | tf_op jit(solution)/shard_map/ppermute | solution.py:14
  462.6 4.1 collective-permute-done.16
  468.6 4.1 collective-permute-done.25
  479.8 4.3 collective-permute-done.26
  491.0 4.7 collective-permute-done.27
  497.4 4.0 collective-permute-done.19
  502.3 4.9 collective-permute-done.28
  516.7 4.3 all-to-all-start.5
  523.4 3.7 all-to-all-done.5
  537.5 6.1 %fusion.130 = bf16[1,512,1024]{2,1,0:T(8,128)(2,1)} fusion(bf16[512,2048]{0,1:T(8,128)(2,1)} %all-gather.9.cloned.1.call-done, bf16[2048,1024]{1,0:T(8,128)(2,1)} %all-gather.11.cloned.1.call-done), kind=kOutput, calls=%fused_computation.151 | convolution fusion | flops 2148007936 | bytes 7340032 | tf_op jit(solution)/shard_map/dot_general | solution.py:180
  (338 shorter events, 159.6 us)
Async XLA Ops:
  7.2 91.5 %copy-start = (bf16[1,512,1024]{2,1,0:T(8,128)(2,1)S(1)}, bf16[1,512,1024]{2,1,0:T(8,128)(2,1)}, u32[]{:S(2)}) copy-start(bf16[1,512,1024]{2,1,0:T(8,128)(2,1)} %param.13) | copy-start | bytes 3145732
  7.2 91.5 %all-gather.11.cloned.1.call-start = ((), (), s32[]{:S(2)}) async-start(), calls=%async_computation.11 | async-start | bytes 4325376 | tf_op jit(solution)/shard_map/all_gather | solution.py:154
  7.9 133.5 %all-gather.5.cloned.1.call-start = ((), (), s32[]{:S(2)}) async-start(), calls=%async_computation.8 | async-start | bytes 1179648 | tf_op jit(solution)/shard_map/all_gather | solution.py:169
  22.3 159.4 %all-gather.7.cloned.1.call-start = ((), (), s32[]{:S(2)}) async-start(), calls=%async_computation.9 | async-start | bytes 1179648 | tf_op jit(solution)/shard_map/all_gather | solution.py:170
  47.5 11.5 %all-to-all-start.1 = ((bf16[4,2,32768]{2,1,0:T(2,128)(2,1)}), bf16[4,2,32768]{2,1,0:T(2,128)(2,1)S(1)}, u32[]{:S(2)}, u32[]{:S(2)}) async-start(bf16[4,2,32768]{2,1,0:T(2,128)(2,1)} %reshape.826), calls=%async_computation.1 | async-start | bytes 1048576 | tf_op jit(solution)/shard_map/all_to_all | solution.py:150
  50.9 199.8 %reduce-scatter.3.cloned.1.call-start = ((), (), s32[]{:S(2)}) async-start(), calls=%async_computation.12 | async-start | bytes 5242880 | tf_op jit(solution)/shard_map/reduce_scatter | solution.py:184
  105.2 76.4 %copy-start.31 = (f32[512,1,4,128]{0,3,2,1:T(8,128)S(1)}, f32[512,1,4,128]{0,3,2,1:T(8,128)}, u32[]{:S(2)}) copy-start(f32[512,1,4,128]{0,3,2,1:T(8,128)} %custom-call.2) | copy-start | bytes 3145732
  105.2 177.7 %all-gather.9.cloned.1.call-start = ((), (), s32[]{:S(2)}) async-start(), calls=%async_computation.10 | async-start | bytes 2621440 | tf_op jit(solution)/shard_map/all_gather | solution.py:179
  253.1 290.5 %reduce-scatter.5.cloned.1.call-start = ((), (), s32[]{:S(2)}) async-start(), calls=%async_computation.13 | async-start | bytes 8650752 | tf_op jit(solution)/shard_map/reduce_scatter | solution.py:191
  291.1 8.5 %collective-permute-start = (bf16[512,1,128]{2,0,1:T(8,128)(2,1)S(1)}, bf16[512,1,128]{2,0,1:T(8,128)(2,1)S(1)}, u32[]{:S(2)}, u32[]{:S(2)}) collective-permute-start(bf16[512,1,128]{2,0,1:T(8,128)(2,1)S(1)} %bitcast.828), channel_id=1, source_target_pairs={{0,4},{4,8},{8,12},{12,16},{16,20},{20,24},{24,28},{28,0},{1,5},{5... | collective-permute-start | bytes 393224 | tf_op jit(solution)/shard_map/ppermute | solution.py:14
  292.6 8.7 %collective-permute-start.1 = (bf16[512,1,128]{2,0,1:T(8,128)(2,1)S(1)}, bf16[512,1,128]{2,0,1:T(8,128)(2,1)S(1)}, u32[]{:S(2)}, u32[]{:S(2)}) collective-permute-start(bf16[512,1,128]{2,0,1:T(8,128)(2,1)S(1)} %bitcast.862), channel_id=1, source_target_pairs={{0,4},{4,8},{8,12},{12,16},{16,20},{20,24},{24,28},{28,0},{1,5},{5... | collective-permute-start | bytes 393224 | tf_op jit(solution)/shard_map/ppermute | solution.py:14
  299.6 11.2 %collective-permute-start.2 = (bf16[512,1,128]{2,0,1:T(8,128)(2,1)S(1)}, bf16[512,1,128]{2,0,1:T(8,128)(2,1)S(1)}, u32[]{:S(2)}, u32[]{:S(2)}) collective-permute-start(bf16[512,1,128]{2,0,1:T(8,128)(2,1)S(1)} %collective-permute-done), channel_id=1, source_target_pairs={{0,4},{4,8},{8,12},{12,16},{16,20},{20,24},{24,28},{28,0},{1,5},{5... | collective-permute-start | bytes 393224 | tf_op jit(solution)/shard_map/ppermute | solution.py:14
  301.3 15.2 %collective-permute-start.3 = (bf16[512,1,128]{2,0,1:T(8,128)(2,1)S(1)}, bf16[512,1,128]{2,0,1:T(8,128)(2,1)S(1)}, u32[]{:S(2)}, u32[]{:S(2)}) collective-permute-start(bf16[512,1,128]{2,0,1:T(8,128)(2,1)S(1)} %collective-permute-done.1), channel_id=1, source_target_pairs={{0,4},{4,8},{8,12},{12,16},{16,20},{20,24},{24,28},{28,0},{1,5},{5... | collective-permute-start | bytes 393224 | tf_op jit(solution)/shard_map/ppermute | solution.py:14
  310.9 11.5 %collective-permute-start.4 = (bf16[512,1,128]{2,0,1:T(8,128)(2,1)S(1)}, bf16[512,1,128]{2,0,1:T(8,128)(2,1)S(1)}, u32[]{:S(2)}, u32[]{:S(2)}) collective-permute-start(bf16[512,1,128]{2,0,1:T(8,128)(2,1)S(1)} %collective-permute-done.2), channel_id=1, source_target_pairs={{0,4},{4,8},{8,12},{12,16},{16,20},{20,24},{24,28},{28,0},{1,5},{5... | collective-permute-start | bytes 393224 | tf_op jit(solution)/shard_map/ppermute | solution.py:14
  316.5 11.5 %collective-permute-start.5 = (bf16[512,1,128]{2,0,1:T(8,128)(2,1)S(1)}, bf16[512,1,128]{2,0,1:T(8,128)(2,1)S(1)}, u32[]{:S(2)}, u32[]{:S(2)}) collective-permute-start(bf16[512,1,128]{2,0,1:T(8,128)(2,1)S(1)} %collective-permute-done.3), channel_id=1, source_target_pairs={{0,4},{4,8},{8,12},{12,16},{16,20},{20,24},{24,28},{28,0},{1,5},{5... | collective-permute-start | bytes 393224 | tf_op jit(solution)/shard_map/ppermute | solution.py:14
  318.1 56.3 %copy-start.3 = (f32[512,512,4]{1,0,2:T(8,128)}, f32[512,512,4]{1,0,2:T(8,128)S(1)}, u32[]{:S(2)}) copy-start(f32[512,512,4]{1,0,2:T(8,128)S(1)} %fusion.240) | copy-start | bytes 12582916
  318.8 57.9 %copy-start.5 = (f32[512,512,4]{1,0,2:T(8,128)}, f32[512,512,4]{1,0,2:T(8,128)S(1)}, u32[]{:S(2)}) copy-start(f32[512,512,4]{1,0,2:T(8,128)S(1)} %fusion.236) | copy-start | bytes 12582916
  322.4 11.5 %collective-permute-start.6 = (bf16[512,1,128]{2,0,1:T(8,128)(2,1)S(1)}, bf16[512,1,128]{2,0,1:T(8,128)(2,1)S(1)}, u32[]{:S(2)}, u32[]{:S(2)}) collective-permute-start(bf16[512,1,128]{2,0,1:T(8,128)(2,1)S(1)} %collective-permute-done.4), channel_id=1, source_target_pairs={{0,4},{4,8},{8,12},{12,16},{16,20},{20,24},{24,28},{28,0},{1,5},{5... | collective-permute-start | bytes 393224 | tf_op jit(solution)/shard_map/ppermute | solution.py:14
  323.1 56.3 %copy-start.6 = (f32[512,512,4]{1,0,2:T(8,128)}, f32[512,512,4]{1,0,2:T(8,128)S(1)}, u32[]{:S(2)}) copy-start(f32[512,512,4]{1,0,2:T(8,128)S(1)} %fusion.232) | copy-start | bytes 12582916
  328.0 11.5 %collective-permute-start.7 = (bf16[512,1,128]{2,0,1:T(8,128)(2,1)S(1)}, bf16[512,1,128]{2,0,1:T(8,128)(2,1)S(1)}, u32[]{:S(2)}, u32[]{:S(2)}) collective-permute-start(bf16[512,1,128]{2,0,1:T(8,128)(2,1)S(1)} %collective-permute-done.5), channel_id=1, source_target_pairs={{0,4},{4,8},{8,12},{12,16},{16,20},{20,24},{24,28},{28,0},{1,5},{5... | collective-permute-start | bytes 393224 | tf_op jit(solution)/shard_map/ppermute | solution.py:14
  333.8 11.8 %collective-permute-start.8 = (bf16[512,1,128]{2,0,1:T(8,128)(2,1)S(1)}, bf16[512,1,128]{2,0,1:T(8,128)(2,1)S(1)}, u32[]{:S(2)}, u32[]{:S(2)}) collective-permute-start(bf16[512,1,128]{2,0,1:T(8,128)(2,1)S(1)} %collective-permute-done.6), channel_id=1, source_target_pairs={{0,4},{4,8},{8,12},{12,16},{16,20},{20,24},{24,28},{28,0},{1,5},{5... | collective-permute-start | bytes 393224 | tf_op jit(solution)/shard_map/ppermute | solution.py:14
  334.9 47.4 %copy-start.8 = (f32[512,512,4]{1,0,2:T(8,128)}, f32[512,512,4]{1,0,2:T(8,128)S(1)}, u32[]{:S(2)}) copy-start(f32[512,512,4]{1,0,2:T(8,128)S(1)} %fusion.228) | copy-start | bytes 12582916
  339.4 11.8 %collective-permute-start.9 = (bf16[512,1,128]{2,0,1:T(8,128)(2,1)S(1)}, bf16[512,1,128]{2,0,1:T(8,128)(2,1)S(1)}, u32[]{:S(2)}, u32[]{:S(2)}) collective-permute-start(bf16[512,1,128]{2,0,1:T(8,128)(2,1)S(1)} %collective-permute-done.7), channel_id=1, source_target_pairs={{0,4},{4,8},{8,12},{12,16},{16,20},{20,24},{24,28},{28,0},{1,5},{5... | collective-permute-start | bytes 393224 | tf_op jit(solution)/shard_map/ppermute | solution.py:14
  345.7 11.5 %collective-permute-start.10 = (bf16[512,1,128]{2,0,1:T(8,128)(2,1)S(1)}, bf16[512,1,128]{2,0,1:T(8,128)(2,1)S(1)}, u32[]{:S(2)}, u32[]{:S(2)}) collective-permute-start(bf16[512,1,128]{2,0,1:T(8,128)(2,1)S(1)} %collective-permute-done.8), channel_id=1, source_target_pairs={{0,4},{4,8},{8,12},{12,16},{16,20},{20,24},{24,28},{28,0},{1,5},{5... | collective-permute-start | bytes 393224 | tf_op jit(solution)/shard_map/ppermute | solution.py:14
  346.4 38.8 %copy-start.10 = (f32[512,512,4]{1,0,2:T(8,128)}, f32[512,512,4]{1,0,2:T(8,128)S(1)}, u32[]{:S(2)}) copy-start(f32[512,512,4]{1,0,2:T(8,128)S(1)} %fusion.224) | copy-start | bytes 12582916
  351.3 11.5 %collective-permute-start.11 = (bf16[512,1,128]{2,0,1:T(8,128)(2,1)S(1)}, bf16[512,1,128]{2,0,1:T(8,128)(2,1)S(1)}, u32[]{:S(2)}, u32[]{:S(2)}) collective-permute-start(bf16[512,1,128]{2,0,1:T(8,128)(2,1)S(1)} %collective-permute-done.9), channel_id=1, source_target_pairs={{0,4},{4,8},{8,12},{12,16},{16,20},{20,24},{24,28},{28,0},{1,5},{5... | collective-permute-start | bytes 393224 | tf_op jit(solution)/shard_map/ppermute | solution.py:14
  357.1 10.6 %collective-permute-start.12 = (bf16[512,1,128]{2,0,1:T(8,128)(2,1)S(1)}, bf16[512,1,128]{2,0,1:T(8,128)(2,1)S(1)}, u32[]{:S(2)}, u32[]{:S(2)}) collective-permute-start(bf16[512,1,128]{2,0,1:T(8,128)(2,1)S(1)} %collective-permute-done.10), channel_id=1, source_target_pairs={{0,4},{4,8},{8,12},{12,16},{16,20},{20,24},{24,28},{28,0},{1,5},{5... | collective-permute-start | bytes 393224 | tf_op jit(solution)/shard_map/ppermute | solution.py:14
  362.7 28.6 %collective-permute-start.13 = (bf16[512,1,128]{2,0,1:T(8,128)(2,1)S(1)}, bf16[512,1,128]{2,0,1:T(8,128)(2,1)S(1)}, u32[]{:S(2)}, u32[]{:S(2)}) collective-permute-start(bf16[512,1,128]{2,0,1:T(8,128)(2,1)S(1)} %collective-permute-done.11), channel_id=1, source_target_pairs={{0,4},{4,8},{8,12},{12,16},{16,20},{20,24},{24,28},{28,0},{1,5},{5... | collective-permute-start | bytes 393224 | tf_op jit(solution)/shard_map/ppermute | solution.py:14
  370.7 49.4 %collective-permute-start.22 = (f32[512,1,128]{0,2,1:T(8,128)}, f32[512,1,128]{0,2,1:T(8,128)}, u32[]{:S(2)}, u32[]{:S(2)}) collective-permute-start(f32[512,1,128]{0,2,1:T(8,128)} %fusion.176), channel_id=1, source_target_pairs={{0,4},{4,8},{8,12},{12,16},{16,20},{20,24},{24,28},{28,0},{1,5},{5... | collective-permute-start | bytes 786440 | tf_op jit(solution)/shard_map/ppermute | solution.py:14
  373.8 51.3 %collective-permute-start.14 = (f32[512,1,128]{2,0,1:T(8,128)}, f32[512,1,128]{2,0,1:T(8,128)}, u32[]{:S(2)}, u32[]{:S(2)}) collective-permute-start(f32[512,1,128]{2,0,1:T(8,128)} %fusion.179), channel_id=1, source_target_pairs={{0,4},{4,8},{8,12},{12,16},{16,20},{20,24},{24,28},{28,0},{1,5},{5... | collective-permute-start | bytes 786440 | tf_op jit(solution)/shard_map/ppermute | solution.py:14
  402.5 114.2 %all-to-all-start.3 = ((bf16[4,2,32768]{2,1,0:T(2,128)(2,1)}), bf16[4,2,32768]{2,1,0:T(2,128)(2,1)S(1)}, u32[]{:S(2)}, u32[]{:S(2)}) async-start(bf16[4,2,32768]{2,1,0:T(2,128)(2,1)} %reshape.830), calls=%async_computation.4 | async-start | bytes 1048576 | tf_op jit(solution)/shard_map/all_to_all | solution.py:230
  423.2 38.7 %copy-start.28 = (bf16[512,1,4,512]{0,3,2,1:T(8,128)(2,1)S(1)}, bf16[512,1,4,512]{0,3,2,1:T(8,128)(2,1)}, u32[]{:S(2)}) copy-start(bf16[512,1,4,512]{0,3,2,1:T(8,128)(2,1)} %copy-done.27) | copy-start | bytes 6291460
  423.2 16.7 %collective-permute-start.23 = (f32[512,1,128]{0,2,1:T(8,128)S(1)}, f32[512,1,128]{0,2,1:T(8,128)S(1)}, u32[]{:S(2)}, u32[]{:S(2)}) collective-permute-start(f32[512,1,128]{0,2,1:T(8,128)S(1)} %fusion.206), channel_id=1, source_target_pairs={{0,4},{4,8},{8,12},{12,16},{16,20},{20,24},{24,28},{28,0},{1,5},{5... | collective-permute-start | bytes 786440 | tf_op jit(solution)/shard_map/ppermute | solution.py:14
  426.8 24.4 %collective-permute-start.15 = (f32[512,1,128]{2,0,1:T(8,128)S(1)}, f32[512,1,128]{2,0,1:T(8,128)S(1)}, u32[]{:S(2)}, u32[]{:S(2)}) collective-permute-start(f32[512,1,128]{2,0,1:T(8,128)S(1)} %fusion.185), channel_id=1, source_target_pairs={{0,4},{4,8},{8,12},{12,16},{16,20},{20,24},{24,28},{28,0},{1,5},{5... | collective-permute-start | bytes 786440 | tf_op jit(solution)/shard_map/ppermute | solution.py:14
  440.0 21.1 %collective-permute-start.24 = (f32[512,1,128]{0,2,1:T(8,128)S(1)}, f32[512,1,128]{0,2,1:T(8,128)S(1)}, u32[]{:S(2)}, u32[]{:S(2)}) collective-permute-start(f32[512,1,128]{0,2,1:T(8,128)S(1)} %add.221), channel_id=1, source_target_pairs={{0,4},{4,8},{8,12},{12,16},{16,20},{20,24},{24,28},{28,0},{1,5},{5... | collective-permute-start | bytes 786440 | tf_op jit(solution)/shard_map/ppermute | solution.py:14
  451.2 15.5 %collective-permute-start.16 = (f32[512,1,128]{2,0,1:T(8,128)S(1)}, f32[512,1,128]{2,0,1:T(8,128)S(1)}, u32[]{:S(2)}, u32[]{:S(2)}) collective-permute-start(f32[512,1,128]{2,0,1:T(8,128)S(1)} %add.214), channel_id=1, source_target_pairs={{0,4},{4,8},{8,12},{12,16},{16,20},{20,24},{24,28},{28,0},{1,5},{5... | collective-permute-start | bytes 786440 | tf_op jit(solution)/shard_map/ppermute | solution.py:14
  461.2 11.4 %collective-permute-start.25 = (f32[512,1,128]{0,2,1:T(8,128)S(1)}, f32[512,1,128]{0,2,1:T(8,128)S(1)}, u32[]{:S(2)}, u32[]{:S(2)}) collective-permute-start(f32[512,1,128]{0,2,1:T(8,128)S(1)} %add.222), channel_id=1, source_target_pairs={{0,4},{4,8},{8,12},{12,16},{16,20},{20,24},{24,28},{28,0},{1,5},{5... | collective-permute-start | bytes 786440 | tf_op jit(solution)/shard_map/ppermute | solution.py:14
  466.8 11.4 %collective-permute-start.17 = (f32[512,1,128]{2,0,1:T(8,128)S(1)}, f32[512,1,128]{2,0,1:T(8,128)S(1)}, u32[]{:S(2)}, u32[]{:S(2)}) collective-permute-start(f32[512,1,128]{2,0,1:T(8,128)S(1)} %add.215), channel_id=1, source_target_pairs={{0,4},{4,8},{8,12},{12,16},{16,20},{20,24},{24,28},{28,0},{1,5},{5... | collective-permute-start | bytes 786440 | tf_op jit(solution)/shard_map/ppermute | solution.py:14
  472.7 11.4 %collective-permute-start.26 = (f32[512,1,128]{0,2,1:T(8,128)S(1)}, f32[512,1,128]{0,2,1:T(8,128)S(1)}, u32[]{:S(2)}, u32[]{:S(2)}) collective-permute-start(f32[512,1,128]{0,2,1:T(8,128)S(1)} %add.223), channel_id=1, source_target_pairs={{0,4},{4,8},{8,12},{12,16},{16,20},{20,24},{24,28},{28,0},{1,5},{5... | collective-permute-start | bytes 786440 | tf_op jit(solution)/shard_map/ppermute | solution.py:14
  478.3 11.4 %collective-permute-start.18 = (f32[512,1,128]{2,0,1:T(8,128)S(1)}, f32[512,1,128]{2,0,1:T(8,128)S(1)}, u32[]{:S(2)}, u32[]{:S(2)}) collective-permute-start(f32[512,1,128]{2,0,1:T(8,128)S(1)} %add.216), channel_id=1, source_target_pairs={{0,4},{4,8},{8,12},{12,16},{16,20},{20,24},{24,28},{28,0},{1,5},{5... | collective-permute-start | bytes 786440 | tf_op jit(solution)/shard_map/ppermute | solution.py:14
  484.2 11.6 %collective-permute-start.27 = (f32[512,1,128]{0,2,1:T(8,128)S(1)}, f32[512,1,128]{0,2,1:T(8,128)S(1)}, u32[]{:S(2)}, u32[]{:S(2)}) collective-permute-start(f32[512,1,128]{0,2,1:T(8,128)S(1)} %add.224), channel_id=1, source_target_pairs={{0,4},{4,8},{8,12},{12,16},{16,20},{20,24},{24,28},{28,0},{1,5},{5... | collective-permute-start | bytes 786440 | tf_op jit(solution)/shard_map/ppermute | solution.py:14
  489.7 11.6 %collective-permute-start.19 = (f32[512,1,128]{2,0,1:T(8,128)S(1)}, f32[512,1,128]{2,0,1:T(8,128)S(1)}, u32[]{:S(2)}, u32[]{:S(2)}) collective-permute-start(f32[512,1,128]{2,0,1:T(8,128)S(1)} %add.217), channel_id=1, source_target_pairs={{0,4},{4,8},{8,12},{12,16},{16,20},{20,24},{24,28},{28,0},{1,5},{5... | collective-permute-start | bytes 786440 | tf_op jit(solution)/shard_map/ppermute | solution.py:14
  495.8 11.4 %collective-permute-start.28 = (f32[512,1,128]{0,2,1:T(8,128)S(1)}, f32[512,1,128]{0,2,1:T(8,128)S(1)}, u32[]{:S(2)}, u32[]{:S(2)}) collective-permute-start(f32[512,1,128]{0,2,1:T(8,128)S(1)} %add.225), channel_id=1, source_target_pairs={{0,4},{4,8},{8,12},{12,16},{16,20},{20,24},{24,28},{28,0},{1,5},{5... | collective-permute-start | bytes 786440 | tf_op jit(solution)/shard_map/ppermute | solution.py:14
  501.4 9.3 %collective-permute-start.20 = (f32[512,1,128]{2,0,1:T(8,128)S(1)}, f32[512,1,128]{2,0,1:T(8,128)S(1)}, u32[]{:S(2)}, u32[]{:S(2)}) collective-permute-start(f32[512,1,128]{2,0,1:T(8,128)S(1)} %add.218), channel_id=1, source_target_pairs={{0,4},{4,8},{8,12},{12,16},{16,20},{20,24},{24,28},{28,0},{1,5},{5... | collective-permute-start | bytes 786440 | tf_op jit(solution)/shard_map/ppermute | solution.py:14
  507.3 7.1 %collective-permute-start.29 = (bf16[512,1,128]{0,2,1:T(8,128)(2,1)S(1)}, bf16[512,1,128]{0,2,1:T(8,128)(2,1)S(1)}, u32[]{:S(2)}, u32[]{:S(2)}) collective-permute-start(bf16[512,1,128]{0,2,1:T(8,128)(2,1)S(1)} %add.226), channel_id=1, source_target_pairs={{0,4},{4,8},{8,12},{12,16},{16,20},{20,24},{24,28},{28,0},{1,5},{5... | collective-permute-start | bytes 393224 | tf_op jit(solution)/shard_map/ppermute | solution.py:14
  510.7 10.3 %collective-permute-start.21 = (bf16[512,1,128]{2,0,1:T(8,128)(2,1)S(1)}, bf16[512,1,128]{2,0,1:T(8,128)(2,1)S(1)}, u32[]{:S(2)}, u32[]{:S(2)}) collective-permute-start(bf16[512,1,128]{2,0,1:T(8,128)(2,1)S(1)} %add.219), channel_id=1, source_target_pairs={{0,4},{4,8},{8,12},{12,16},{16,20},{20,24},{24,28},{28,0},{1,5},{5... | collective-permute-start | bytes 393224 | tf_op jit(solution)/shard_map/ppermute | solution.py:14
  516.7 10.4 %all-to-all-start.5 = ((bf16[4,2,8192]{2,1,0:T(2,128)(2,1)}), bf16[4,2,8192]{2,1,0:T(2,128)(2,1)S(1)}, u32[]{:S(2)}, u32[]{:S(2)}) async-start(bf16[4,2,8192]{2,1,0:T(2,128)(2,1)} %reshape.834), calls=%async_computation.6 | async-start | bytes 262144 | tf_op jit(solution)/shard_map/all_to_all | solution.py:232
  527.1 9.3 %all-to-all-start.4 = ((bf16[4,2,8192]{2,1,0:T(2,128)(2,1)}), bf16[4,2,8192]{2,1,0:T(2,128)(2,1)S(1)}, u32[]{:S(2)}, u32[]{:S(2)}) async-start(bf16[4,2,8192]{2,1,0:T(2,128)(2,1)} %reshape.832), calls=%async_computation.5 | async-start | bytes 262144 | tf_op jit(solution)/shard_map/all_to_all | solution.py:231
  (54 other events, 428.4 us)
Sparse Core Ops, SparseCore 0:
  9.7 88.9 all-gather.10
  100.9 40.5 all-gather.4
  143.6 37.9 all-gather.6
  183.9 45.7 reduce-scatter.2
  253.2 29.7 all-gather.8
  290.4 175.4 reduce-scatter.4
where the time goes:
time: 560 us; the launch traced here: 551 us
  waiting for transfers between devices  284 us (51%)
  matrix products  123 us (22%)
  starting transfers between devices  41.9 us (7%)
  other arithmetic  37.6 us (7%)
  local copies, waits for them, and re-layouts  30.1 us (5%)
  blocking collectives  18.5 us (3%)
  between operations  15.6 us (3%)
    ppermute x30, waiting for transfers between devices, from_behind(): lax.ppermute(array, axis, [(i, (i + by) % length) for i in range(length)])  127 us
    all_gather x1, waiting for transfers between devices, shards(): lax.all_gather(value_heads, 'blk', axis=1, tiled=True)[0]  40.2 us
    all_gather x1, waiting for transfers between devices, shards(): weight_whole = lax.all_gather(out_weight, ('dp', 'blk'), axis=0, tiled=True)  38.6 us
    all_gather x1, waiting for transfers between devices, shards(): lax.all_gather(key_heads, 'blk', axis=1, tiled=True)[0]  35.9 us
    dot_general x16, matrix products, score_tile(): jnp.einsum('qcgd,kcd->qcgk', query_groups, key_block, preferred_element_t...  35.9 us
    all_gather x1, waiting for transfers between devices, shards(): lax.all_gather(attention_rows, 'ulysses', axis=1, tiled=True)  29.8 us
    dot_general x8, matrix products, forward_tile(): jnp.einsum('qcgk,kcd->qcgd', weights.astype(jnp.bfloat16), value_block, p...  28.9 us
    ppermute x30, starting transfers between devices, from_behind(): lax.ppermute(array, axis, [(i, (i + by) % length) for i in range(length)])  26.9 us
  transfers between devices with their start and end apart: 40, of which 33 were waited for; matrix products, arithmetic and copies ran while one was open for 31% of the time, Pallas kernels for 0%

commit v1 on v0

v1 whole, which is shorter than its diff:
```python
import functools
import math

import jax
import jax.numpy as jnp
from jax import lax
from jax.experimental import pallas as pl
from jax.experimental.pallas import tpu as pltpu
from jax.sharding import Mesh
from jax.sharding import PartitionSpec as P

HD = 128
GROUP = 4
SEG = 256
SCALE = HD ** (-0.5)
LOG2_SCALE = SCALE * math.log2(math.e)
MASKED = -1e30
BF16 = jnp.bfloat16
F32 = jnp.float32
VMEM_LIMIT = 48 * 1024 * 1024
PLANE = ("zhi", "zlo", "y")
BLOCK = ("zlo", "y")


def dot(a, b):
    return jnp.dot(a, b, preferred_element_type=F32)


def dot_nt(a, b):
    return lax.dot_general(a, b, (((1,), (1,)), ((), ())), preferred_element_type=F32)


def diagonal_mask():
    key_index = lax.broadcasted_iota(jnp.int32, (SEG, SEG), 0)
    query_index = lax.broadcasted_iota(jnp.int32, (SEG, SEG), 1)
    return key_index <= query_index


def forward_kernel(
    order_ref, rank_ref, q_ref, kv_ref, att_ref, att_t_ref, lse_ref, q_t, v_t, acc, peak, total
):
    runs = q_ref.shape[0] // SEG
    heads = q_ref.shape[1] // HD
    key_runs = kv_ref.shape[0] // SEG

    q_t[...] = q_ref[...].T

    @pl.loop(0, key_runs)
    def _(j):
        rows = pl.ds(pl.multiple_of(j * SEG, SEG), SEG)
        v_t[j] = kv_ref[rows, HD:].T

    for run in range(runs):
        cols = pl.ds(run * SEG, SEG)
        rank = rank_ref[run]

        def tiles(indexes, first):
            keys = [kv_ref[pl.ds(pl.multiple_of(j * SEG, SEG), SEG), :HD] for j in indexes]
            values = [v_t[j] for j in indexes]
            for h in range(heads):
                queries = q_t[pl.ds(h * HD, HD), cols]
                scores = [dot(k, queries) for k in keys]
                if first:
                    mask = diagonal_mask()
                    scores = [jnp.where(mask, s, MASKED) for s in scores]
                top = functools.reduce(
                    jnp.maximum, [jnp.max(s, axis=0, keepdims=True) for s in scores]
                )
                if not first:
                    old = peak[pl.ds(h, 1), :]
                    top = jnp.maximum(top, old)
                shift = top * LOG2_SCALE
                weights = [jnp.exp2(s * LOG2_SCALE - shift) for s in scores]
                summed = functools.reduce(
                    jnp.add, [jnp.sum(w, axis=0, keepdims=True) for w in weights]
                )
                mixed = functools.reduce(
                    jnp.add, [dot(v, w.astype(BF16)) for v, w in zip(values, weights)]
                )
                if first:
                    total[pl.ds(h, 1), :] = summed
                    acc[pl.ds(h * HD, HD), :] = mixed
                else:
                    factor = jnp.exp2(old * LOG2_SCALE - shift)
                    total[pl.ds(h, 1), :] = total[pl.ds(h, 1), :] * factor + summed
                    acc[pl.ds(h * HD, HD), :] = acc[pl.ds(h * HD, HD), :] * factor + mixed
                peak[pl.ds(h, 1), :] = top

        tiles([order_ref[rank]], True)

        @pl.loop(0, rank // 2)
        def _(pair):
            tiles([order_ref[2 * pair], order_ref[2 * pair + 1]], False)

        @pl.when(rank % 2 == 1)
        def _():
            tiles([order_ref[rank - 1]], False)

        for h in range(heads):
            row_total = total[pl.ds(h, 1), :]
            lse_ref[pl.ds(h, 1), cols] = peak[pl.ds(h, 1), :] * LOG2_SCALE + jnp.log2(row_total)
            out = (acc[pl.ds(h * HD, HD), :] / row_total).astype(BF16)
            att_t_ref[pl.ds(h * HD, HD), cols] = out
            att_ref[cols, pl.ds(h * HD, HD)] = out.T


def attend(order, rank, q, kv):
    rows, width = q.shape
    heads = width // HD
    length = kv.shape[0]
    smem = pl.BlockSpec(memory_space=pltpu.SMEM)
    vmem = pl.BlockSpec(memory_space=pltpu.VMEM)
    return pl.pallas_call(
        forward_kernel,
        name="attention_forward",
        out_shape=(
            jax.ShapeDtypeStruct((rows, width), BF16),
            jax.ShapeDtypeStruct((width, rows), BF16),
            jax.ShapeDtypeStruct((heads, rows), F32),
        ),
        in_specs=[smem, smem, vmem, vmem],
        out_specs=(vmem, vmem, vmem),
        scratch_shapes=[
            pltpu.VMEM((width, rows), BF16),
            pltpu.VMEM((length // SEG, HD, SEG), BF16),
            pltpu.VMEM((width, SEG), F32),
            pltpu.VMEM((8, SEG), F32),
            pltpu.VMEM((8, SEG), F32),
        ],
        compiler_params=pltpu.CompilerParams(vmem_limit_bytes=VMEM_LIMIT),
        cost_estimate=pl.CostEstimate(
            flops=4 * rows * length * width,
            bytes_accessed=2 * (3 * rows * width + length * 2 * HD),
            transcendentals=rows * length * heads,
        ),
    )(order, rank, q, kv)


def backward_kernel(
    rank_ref,
    key_rank_ref,
    q_ref,
    kv_ref,
    grad_t_ref,
    att_t_ref,
    lse_ref,
    dq_ref,
    dkv_ref,
    q_t,
    grad,
    delta,
    dq_t,
    dk,
    dv,
):
    runs = q_ref.shape[0] // SEG
    heads = q_ref.shape[1] // HD
    key_runs = kv_ref.shape[0] // SEG

    q_t[...] = q_ref[...].T
    grad[...] = grad_t_ref[...].T
    dq_t[...] = jnp.zeros_like(dq_t)
    for h in range(heads):
        part = pl.ds(h * HD, HD)
        delta[pl.ds(h, 1), :] = jnp.sum(
            grad_t_ref[part, :].astype(F32) * att_t_ref[part, :].astype(F32),
            axis=0,
            keepdims=True,
        )

    @pl.loop(0, key_runs)
    def _(j):
        rows = pl.ds(pl.multiple_of(j * SEG, SEG), SEG)
        key_rank = key_rank_ref[j]
        dk[...] = jnp.zeros_like(dk)
        dv[...] = jnp.zeros_like(dv)

        def tile(run, masked):
            cols = pl.ds(run * SEG, SEG)
            keys = kv_ref[rows, :HD]
            values = kv_ref[rows, HD:]
            keys_t = keys.T
            dk_now = dk[...]
            dv_now = dv[...]
            for h in range(heads):
                part = pl.ds(h * HD, HD)
                scores = dot(keys, q_t[part, cols])
                probs = jnp.exp2(scores * LOG2_SCALE - lse_ref[pl.ds(h, 1), cols])
                if masked:
                    probs = jnp.where(diagonal_mask(), probs, 0.0)
                prob_grad = dot(values, grad_t_ref[part, cols])
                score_grad = (probs * (prob_grad - delta[pl.ds(h, 1), cols])).astype(BF16)
                dv_now = dv_now + dot(probs.astype(BF16), grad[cols, part])
                dk_now = dk_now + dot(score_grad, q_ref[cols, part])
                dq_t[part, cols] += dot(keys_t, score_grad)
            dk[...] = dk_now
            dv[...] = dv_now

        for run in range(runs):
            pl.when(key_rank < rank_ref[run])(functools.partial(tile, run, False))
            pl.when(key_rank == rank_ref[run])(functools.partial(tile, run, True))
        dkv_ref[rows, :HD] = (dk[...] * SCALE).astype(BF16)
        dkv_ref[rows, HD:] = dv[...].astype(BF16)

    for run in range(runs):
        cols = pl.ds(run * SEG, SEG)
        for h in range(heads):
            part = pl.ds(h * HD, HD)
            dq_ref[cols, part] = (dq_t[part, cols] * SCALE).astype(BF16).T


def attend_back(rank, key_rank, q, kv, grad_t, att_t, lse):
    rows, width = q.shape
    heads = width // HD
    length = kv.shape[0]
    smem = pl.BlockSpec(memory_space=pltpu.SMEM)
    vmem = pl.BlockSpec(memory_space=pltpu.VMEM)
    return pl.pallas_call(
        backward_kernel,
        name="attention_backward",
        out_shape=(
            jax.ShapeDtypeStruct((rows, width), BF16),
            jax.ShapeDtypeStruct((length, 2 * HD), BF16),
        ),
        in_specs=[smem, smem] + [vmem] * 5,
        out_specs=(vmem, vmem),
        scratch_shapes=[
            pltpu.VMEM((width, rows), BF16),
            pltpu.VMEM((rows, width), BF16),
            pltpu.VMEM((8, rows), F32),
            pltpu.VMEM((width, rows), F32),
            pltpu.VMEM((SEG, HD), F32),
            pltpu.VMEM((SEG, HD), F32),
        ],
        compiler_params=pltpu.CompilerParams(vmem_limit_bytes=VMEM_LIMIT),
        cost_estimate=pl.CostEstimate(
            flops=10 * rows * length * width,
            bytes_accessed=2 * (4 * rows * width + 2 * length * 2 * HD),
            transcendentals=rows * length * heads,
        ),
    )(rank, key_rank, q, kv, grad_t, att_t, lse)


def pack_kernel(q_ref, k_ref, v_ref, out_ref):
    parts, _, total = out_ref.shape
    width = total - 2 * HD
    for i in range(parts):
        out_ref[i, :, :width] = q_ref[0, :, pl.ds(i * width, width)]
        out_ref[i, :, width : width + HD] = k_ref[0, :, pl.ds(i * HD, HD)]
        out_ref[i, :, width + HD :] = v_ref[0, :, pl.ds(i * HD, HD)]


def pack(queries, key_vectors, value_vectors):
    own = queries.shape[1]
    parts = key_vectors.shape[2] // HD
    width = queries.shape[2] // parts
    return pl.pallas_call(
        pack_kernel,
        name="pack_heads",
        out_shape=jax.ShapeDtypeStruct((parts, own, width + 2 * HD), BF16),
    )(queries, key_vectors, value_vectors)


def finish_kernel(source_ref, *refs):
    pieces, dkv_ref, (dq_ref, dk_ref, dv_ref) = refs[:-4], refs[-4], refs[-3:]
    width = pieces[0].shape[1]
    for i, piece in enumerate(pieces):
        columns = pl.ds(pl.multiple_of(source_ref[i] * width, width), width)
        dq_ref[0, :, columns] = piece[...]
    blocks, parts = dkv_ref.shape[:2]
    for u in range(parts):
        total = dkv_ref[0, u].astype(F32)
        for b in range(1, blocks):
            total = total + dkv_ref[b, u].astype(F32)
        total = total.astype(BF16)
        dk_ref[0, :, pl.ds(u * HD, HD)] = total[:, :HD]
        dv_ref[0, :, pl.ds(u * HD, HD)] = total[:, HD:]


def finish(source, pieces, dkv):
    own, width = pieces[0].shape
    parts = len(pieces)
    smem = pl.BlockSpec(memory_space=pltpu.SMEM)
    vmem = pl.BlockSpec(memory_space=pltpu.VMEM)
    return pl.pallas_call(
        finish_kernel,
        name="gather_gradients",
        in_specs=[smem] + [vmem] * (parts + 1),
        out_specs=(vmem, vmem, vmem),
        out_shape=(
            jax.ShapeDtypeStruct((1, own, parts * width), BF16),
            jax.ShapeDtypeStruct((1, own, parts * HD), BF16),
            jax.ShapeDtypeStruct((1, own, parts * HD), BF16),
        ),
        compiler_params=pltpu.CompilerParams(vmem_limit_bytes=VMEM_LIMIT),
    )(source, *pieces, dkv)


def exchange(array, axes):
    return lax.all_to_all(array, axes, split_axis=0, concat_axis=0, tiled=True)


def shift(array, axis, by):
    length = lax.axis_size(axis)
    return lax.ppermute(array, axis, [(i, (i + by) % length) for i in range(length)])


def pick(array, index):
    return lax.dynamic_index_in_dim(array, index, 0, keepdims=False)


def put(array, piece, index):
    return lax.dynamic_update_index_in_dim(array, piece, index, 0)


def swap_pairs(by):
    pairs = []
    for zhi in range(2):
        for core in range(2):
            for y in range(4):
                for x in range(4):
                    source = ((zhi * 2 + core) * 4 + y) * 4 + x
                    target = (((x % 2) * 2 + x // 2) * 4 + (y + by) % 4) * 4 + zhi * 2 + core
                    pairs.append((source, target))
    return pairs


def swap(array, by):
    return lax.ppermute(array, ("zhi", "core", "y", "x"), swap_pairs(by))


def swap_back(array):
    return lax.ppermute(array, ("zhi", "core", "y", "x"), [(b, a) for a, b in swap_pairs(0)])


def after(array, *others):
    return lax.optimization_barrier((array,) + others)[0]


def shards(queries, key_vectors, value_vectors, positions, out_weight, out_grad):
    x = lax.axis_index("x")
    y = lax.axis_index("y")
    z = lax.axis_index(("zhi", "zlo"))
    core = lax.axis_index("core")
    blk = lax.axis_index(BLOCK)
    xs = lax.axis_size("x")
    own = queries.shape[1]
    width = queries.shape[2] // xs
    blocks = lax.axis_size(BLOCK)
    rows = own * xs
    columns = out_grad.shape[2]

    key_rank = positions[0, ::SEG] // SEG
    count = key_rank.shape[0]
    index = jnp.arange(count, dtype=jnp.int32)
    order = jnp.sum(
        jnp.where(key_rank[None, :] == index[:, None], index[None, :], 0), axis=1
    ).astype(jnp.int32)
    rank = lax.dynamic_slice_in_dim(key_rank, blk * (rows // SEG), rows // SEG)

    og = lax.all_gather(out_grad[0], "x", axis=0)

    along_y = jnp.zeros((4,) + out_weight.shape, BF16)
    for d in range(4):
        along_y = put(along_y, swap(out_weight, d), (y - d) % 4)
    along_z = put(jnp.zeros((4,) + along_y.shape, BF16), along_y, z)
    for d in range(1, 4):
        along_z = put(along_z, shift(along_y, ("zhi", "zlo"), d), (z - d) % 4)
    weight = put(jnp.zeros((2,) + along_z.shape, BF16), along_z, core)
    weight = put(weight, shift(along_z, "core", 1), 1 - core)
    weight = weight.reshape(xs, width, columns)

    qkv = exchange(pack(queries, key_vectors, value_vectors), "x").reshape(rows, width + 2 * HD)
    q, kv_block = qkv[:, :width], qkv[:, width:]

    kv = exchange(jnp.broadcast_to(kv_block[None], (blocks,) + kv_block.shape), BLOCK)
    kv = kv.reshape(blocks * rows, 2 * HD)

    att, att_t, lse = attend(order, rank, q, kv)

    og_half = og.reshape(2, 2, rows, columns)

    def weight_part(half):
        return jnp.einsum("ft,ztc->zfc", att_t, pick(og_half, half), preferred_element_type=F32)

    wg_got = shift(weight_part(1 - core).astype(BF16), "core", 1)
    wg_half = (weight_part(core) + wg_got.astype(F32)).astype(BF16)
    wg_half = wg_half.reshape(2 * blocks, width // blocks, columns)
    wg_parts = exchange(wg_half, PLANE)
    weight_grad = swap_back(jnp.sum(wg_parts.astype(F32), axis=0))

    grad_t = jnp.einsum("gfc,gtc->ft", weight, og, preferred_element_type=F32).astype(BF16)

    lo = jnp.einsum("tf,gfc->gtc", att, weight, preferred_element_type=F32).astype(BF16)
    layer_output = lax.psum_scatter(lo, "x", scatter_dimension=0, tiled=True)

    grad_t = after(grad_t, wg_half, lo)
    dq, dkv = attend_back(rank, key_rank, q, kv, grad_t, att_t, lse)

    dq_parts = dq.reshape(xs, own, width)
    pieces = [pick(dq_parts, x)]
    for d in range(1, xs):
        pieces.append(shift(pick(dq_parts, (x + d) % xs), "x", d))
    source = jnp.stack([(x - d) % xs for d in range(xs)]).astype(jnp.int32)
    dkv_got = exchange(dkv.reshape(blocks * xs, own, 2 * HD), BLOCK + ("x",))
    dkv_got = dkv_got.reshape(blocks, xs, own, 2 * HD)
    query_grad, key_grad, value_grad = finish(source, pieces, dkv_got)
    return (layer_output, query_grad, key_grad, value_grad, weight_grad)


def solution(mesh):
    split = Mesh(mesh.devices.reshape(2, 2, 2, 4, 4), ("zhi", "core", "zlo", "y", "x"))
    dp = ("zhi", "core")
    tokens = P(dp, ("zlo", "y", "x"), None)
    weight = P(("zhi", "core", "zlo", "y"), "x")
    columns = P(dp, BLOCK, "x")
    return jax.shard_map(
        shards,
        mesh=split,
        in_specs=(tokens, tokens, tokens, P(dp, None), weight, columns),
        out_specs=(columns, tokens, tokens, tokens, weight),
        check_vma=False,
    )
```

time: 560 us -> 238 us (0.42); the launches traced: 551 us -> 236 us
  waiting for transfers between devices: 284 us -> 46.5 us
  matrix products: 123 us -> 18.1 us
  starting transfers between devices: 41.9 us -> 86.1 us
  Pallas kernels: 0 us -> 43.4 us
  other arithmetic: 37.6 us -> 2.22 us
  blocking collectives: 18.5 us -> 0 us
    all_gather x4 -> x1, waiting for transfers between devices: 145 us -> 0.02 us  [shards(): og = lax.all_gather(out_grad[0], 'x', axis=0)]
    ppermute x30 -> x13, waiting for transfers between devices: 127 us -> 21.9 us  [the longest x8 21.8 us: shift(): lax.ppermute(array, axis, [(i, (i + by) % length) for i in range(length)])]
    dot_general x59 -> x4, matrix products: 123 us -> 18.1 us  [the longest x1 6.63 us: shards(): jnp.einsum('tf,gfc->gtc', att, weight, preferred_element_type=F32)]
    pallas_call x0 -> x4, Pallas kernels: none -> 43.4 us  [the longest x1 21.9 us: attend_back(): pl.pallas_call(backward_kernel, name='attention_backward', out_shape=(jax...]
    all_to_all x4, starting transfers between devices: 14.5 us -> 52.8 us  [exchange(): return lax.all_to_all(array, axes, split_axis=0, concat_axis=0, tiled=True)]
    unnamed x10 -> x0, other arithmetic: 22.9 us -> none
    unnamed x135 -> x14, local copies, waits for them, and re-layouts: 25 us -> 5.31 us
    all_to_all x2 -> x0, blocking collectives: 18.5 us -> none  [the longest x1 10.2 us: shards(): lax.all_to_all(key_vectors, 'ulysses', split_axis=2, concat_axis=1, tiled...]
  transfers between devices with their start and end apart: 40 -> 19, of which waited for: 33 -> 6; matrix products, arithmetic and copies ran while one was open for 31% -> 17% of each run, Pallas kernels for 0% -> 18%
where the time goes in v1:
time: 238 us; the launch traced here: 236 us
  starting transfers between devices  86.1 us (36%)
  waiting for transfers between devices  46.5 us (20%)
  Pallas kernels  43.4 us (18%)
  local copies, waits for them, and re-layouts  25.9 us (11%)
  matrix products  18.1 us (8%)
  between operations  14.3 us (6%)
    all_to_all x4, starting transfers between devices, exchange(): return lax.all_to_all(array, axes, split_axis=0, concat_axis=0, tiled=True)  52.8 us
    ppermute x8, starting transfers between devices, shift(): lax.ppermute(array, axis, [(i, (i + by) % length) for i in range(length)])  25 us
    all_to_all x4, waiting for transfers between devices, exchange(): return lax.all_to_all(array, axes, split_axis=0, concat_axis=0, tiled=True)  24 us
    pallas_call x1, Pallas kernels, attend_back(): pl.pallas_call(backward_kernel, name='attention_backward', out_shape=(jax...  21.9 us
    ppermute x8, waiting for transfers between devices, shift(): lax.ppermute(array, axis, [(i, (i + by) % length) for i in range(length)])  21.8 us
    pallas_call x1, Pallas kernels, attend(): pl.pallas_call(forward_kernel, name='attention_forward', out_shape=(jax.S...  17.9 us
    dynamic_update_slice x10, local copies, waits for them, and re-layouts, put(): return lax.dynamic_update_index_in_dim(array, piece, index, 0)  12.1 us
    ppermute x4, starting transfers between devices, swap(): return lax.ppermute(array, ('zhi', 'core', 'y', 'x'), swap_pairs(by))  7.47 us
  transfers between devices with their start and end apart: 19, of which 6 were waited for; matrix products, arithmetic and copies ran while one was open for 17% of the time, Pallas kernels for 18%

profile of v1, /device:TPU:0, one launch (start us, length us, event | category | flops | bytes accessed | tf_op | source)
XLA Modules:
  0.0 236.5 jit_solution(5957429779247294231)
XLA Ops:
  7.2 0.7 all-gather.2.cloned.1.call-update
  7.9 1.6 collective-permute-start
  9.5 1.7 collective-permute-start.1
  11.1 2.9 %collective-permute-start.2 = (bf16[64,1024]{1,0:T(8,128)(2,1)}, bf16[64,1024]{1,0:T(8,128)(2,1)S(1)}, u32[]{:S(2)}, u32[]{:S(2)}) collective-permute-start(bf16[64,1024]{1,0:T(8,128)(2,1)} %param.10), channel_id=1, source_target_pairs={{0,8},{1,72},{2,40},{3,104},{4,12},{5,76},{6,44},{7,108},{8,0},{9,... | collective-permute-start | bytes 393224 | tf_op jit(solution)/shard_map/ppermute | solution.py:329
  14.0 1.3 collective-permute-start.3
  15.4 2.1 pack_heads.1
  17.5 13.5 %all-to-all-start = ((bf16[4,128,768]{2,1,0:T(8,128)(2,1)}), bf16[4,128,768]{2,1,0:T(8,128)(2,1)S(1)}, u32[]{:S(2)}, u32[]{:S(2)}) async-start(bf16[4,128,768]{2,1,0:T(8,128)(2,1)} %pack_heads.1), calls=%async_computation | async-start | bytes 1572864 | tf_op jit(solution)/shard_map/all_to_all | solution.py:300
  31.1 2.0 collective-permute-start.4
  33.1 0.9 collective-permute-start.5
  34.0 1.9 collective-permute-start.6
  35.9 1.6 broadcast_in_dim.64
  37.5 0.8 bitcast_dynamic-update-slice_fusion.5
  38.3 13.2 %all-to-all-done = bf16[4,128,768]{2,1,0:T(8,128)(2,1)S(1)} async-done(((bf16[4,128,768]{2,1,0:T(8,128)(2,1)}), bf16[4,128,768]{2,1,0:T(8,128)(2,1)S(1)}, u32[]{:S(2)}, u32[]{:S(2)}) %all-to-all-start) | async-done | bytes 786464 | tf_op jit(solution)/shard_map/all_to_all | solution.py:300
  51.5 1.6 broadcast_in_dim.78
  53.1 3.6 %all-to-all-start.1 = ((bf16[8,512,256]{2,1,0:T(8,128)(2,1)}), bf16[8,512,256]{2,1,0:T(8,128)(2,1)S(1)}, u32[]{:S(2)}, u32[]{:S(2)}) async-start(bf16[8,512,256]{2,1,0:T(8,128)(2,1)} %broadcast_in_dim.78), calls=%async_computation.1 | async-start | bytes 4194304 | tf_op jit(solution)/shard_map/all_to_all | solution.py:300
  56.8 1.9 bitcast_dynamic-update-slice_fusion.4
  58.7 0.9 bitcast_dynamic-update-slice_fusion.3
  59.6 1.9 bitcast_dynamic-update-slice_fusion.2
  61.4 6.1 %collective-permute-start.7 = (bf16[4,4,64,1024]{3,2,1,0:T(8,128)(2,1)}, bf16[4,4,64,1024]{3,2,1,0:T(8,128)(2,1)}, u32[]{:S(2)}, u32[]{:S(2)}) collective-permute-start(bf16[4,4,64,1024]{3,2,1,0:T(8,128)(2,1)} %bitcast_dynamic-update-slice_fusion.2), channel_id=1, source_target_pairs={{0,32},{32,0},{1,33},{33,1},{2,34},{34,2},{3,35},{35,3},{4,36},{36... | collective-permute-start | bytes 6291464 | tf_op jit(solution)/shard_map/ppermute | solution.py:305
  67.5 0.8 slice.9
  68.5 1.1 slice.12.q_ref
  69.6 2.5 %broadcast_in_dim.63 = bf16[2,4,4,64,1024]{4,3,2,1,0:T(8,128)(2,1)} broadcast(bf16[]{:T(256)} %constant.149.clone.1), dimensions={} | broadcast | bytes 4194306 | tf_op jit(solution)/shard_map/broadcast_in_dim | solution.py:369
  72.1 3.2 %bitcast_dynamic-update-slice_fusion.1 = bf16[2,4,4,64,1024]{4,3,2,1,0:T(8,128)(2,1)} fusion(bf16[2,4,4,64,1024]{4,3,2,1,0:T(8,128)(2,1)} %broadcast_in_dim.63, s32[]{:T(128)S(6)} %select_n.137, bf16[4,4,64,1024]{3,2,1,0:T(8,128)(2,1)} %bitcast_dynamic-update-slice_fusion.2), kind=kLoop, calls=%fused_computation.8 | loop fusion | bytes 4194308 | tf_op jit(solution)/shard_map/jit(dynamic_update_index_in_dim)/dynamic_update_slice | solution.py:313
  75.4 6.0 %all-to-all-done.1 = bf16[8,512,256]{2,1,0:T(8,128)(2,1)S(1)} async-done(((bf16[8,512,256]{2,1,0:T(8,128)(2,1)}), bf16[8,512,256]{2,1,0:T(8,128)(2,1)S(1)}, u32[]{:S(2)}, u32[]{:S(2)}) %all-to-all-start.1) | async-done | bytes 2097184 | tf_op jit(solution)/shard_map/all_to_all | solution.py:300
  81.4 17.9 %attention_forward.1 = (bf16[512,512]{1,0:T(8,128)(2,1)S(1)}, bf16[512,512]{1,0:T(8,128)(2,1)S(1)}, f32[4,512]{1,0:T(4,128)S(1)}) custom-call(s32[16]{0:T(128)S(1)} %select_reduce_fusion.order_ref, s32[2]{0:T(128)S(1)} %dynamic_slice.23.rank_ref, bf16[512,512]{1,0:T(8,128)(2,1)S(1)} %slice.12.q_ref, bf16[4096,256]{1,0:T(8,128)(2,1)S(1)} %bitcast.84), custom_call_target="tpu_custom_call" | custom-call | flops 4294967296 | bytes 3670016 | tf_op jit(solution)/shard_map/attention_forward/pallas_call | solution.py:113
  99.3 3.4 %bitcast_dynamic-update-slice_fusion = bf16[2,4,4,64,1024]{4,3,2,1,0:T(8,128)(2,1)} fusion(bf16[2,4,4,64,1024]{4,3,2,1,0:T(8,128)(2,1)} %bitcast_dynamic-update-slice_fusion.1, s32[]{:T(128)S(6)} %select_n.138, bf16[4,4,64,1024]{3,2,1,0:T(8,128)(2,1)} %collective-permute-done.7), kind=kLoop, calls=%fused_computation.7 | loop fusion | bytes 4194308 | tf_op jit(solution)/shard_map/jit(dynamic_update_index_in_dim)/dynamic_update_slice | solution.py:313
  102.7 6.6 %convert_bitcast_fusion = bf16[4,512,1024]{1,2,0:T(8,128)(2,1)} fusion(bf16[4,512,1024]{2,1,0:T(8,128)(2,1)} %bitcast.10, bf16[512,512]{1,0:T(8,128)(2,1)S(1)} %get-tuple-element.14), kind=kOutput, calls=%fused_computation.3 | convolution fusion | flops 2149580800 | bytes 8912896 | tf_op jit(solution)/shard_map/tf,gfc->gtc/dot_general | solution.py:394
  109.4 1.0 copy-done.3
  110.3 3.0 %convert_bitcast_fusion.1 = bf16[2,512,1024]{2,1,0:T(8,128)(2,1)S(1)} fusion(bf16[2,2,512,1024]{3,2,1,0:T(8,128)(2,1)} %bitcast.90, s32[]{:T(128)S(6)} %select_n.138, bf16[512,512]{1,0:T(8,128)(2,1)S(1)} %copy-done.3), kind=kOutput, calls=%fused_computation.9 | convolution fusion | flops 1074790400 | bytes 4718596 | tf_op jit(solution)/shard_map/ft,ztc->zfc/dot_general | solution.py:384
  113.4 0.8 collective-permute-start.8
  114.2 3.8 %collective-permute-done.8 = bf16[2,512,1024]{2,1,0:T(8,128)(2,1)S(1)} collective-permute-done((bf16[2,512,1024]{2,1,0:T(8,128)(2,1)S(1)}, bf16[2,512,1024]{2,1,0:T(8,128)(2,1)S(1)}, u32[]{:S(2)}, u32[]{:S(2)}) %collective-permute-start.8) | collective-permute-done | bytes 2097184 | tf_op jit(solution)/shard_map/ppermute | solution.py:305
  118.0 2.6 %fusion = bf16[2,512,1024]{2,1,0:T(8,128)(2,1)} fusion(bf16[2,512,1024]{2,1,0:T(8,128)(2,1)S(1)} %collective-permute-done.8, bf16[2,2,512,1024]{3,2,1,0:T(8,128)(2,1)S(1)} %bitcast.91, s32[]{:T(128)S(6)} %select_n.137, bf16[512,512]{1,0:T(8,128)(2,1)S(1)} %copy-done.3), kind=kOutput, calls=%fused_computation.1 | convolution fusion | flops 1076887552 | bytes 6815748 | tf_op jit(solution)/shard_map/ft,ztc->zfc/dot_general | solution.py:384
  120.6 20.1 %all-to-all-start.3 = ((bf16[16,64,1024]{2,1,0:T(8,128)(2,1)}), bf16[16,64,1024]{2,1,0:T(8,128)(2,1)}, u32[]{:S(2)}, u32[]{:S(2)}) async-start(bf16[16,64,1024]{2,1,0:T(8,128)(2,1)} %bitcast.89), calls=%async_computation.4 | async-start | bytes 4194304 | tf_op jit(solution)/shard_map/all_to_all | solution.py:300
  140.7 5.8 %fusion.8.grad_t_ref = bf16[512,512]{1,0:T(8,128)(2,1)S(1)} fusion(bf16[4,512,1024]{2,1,0:T(8,128)(2,1)} %bitcast.10, bf16[4,512,1024]{2,1,0:T(8,128)(2,1)} %all-gather.2.cloned.1.call-done), kind=kOutput, calls=%fused_computation.13 | convolution fusion | flops 2147745792 | bytes 8912896 | tf_op jit(solution)/shard_map/gfc,gtc->ft/dot_general | solution.py:392
  146.5 21.9 %attention_backward.1 = (bf16[512,512]{1,0:T(8,128)(2,1)S(1)}, bf16[4096,256]{1,0:T(8,128)(2,1)S(1)}) custom-call(s32[2]{0:T(128)S(1)} %dynamic_slice.23.rank_ref, s32[16]{0:T(128)S(1)} %and_select_fusion.key_rank_ref, bf16[512,512]{1,0:T(8,128)(2,1)S(1)} %slice.12.q_ref, bf16[4096,256]{1,0:T(8,128)(2,1)} %bitcast.85, ...), custom_call_target="tpu_custom_call" | custom-call | flops 10737418240 | bytes 6291456 | tf_op jit(solution)/shard_map/attention_backward/pallas_call | solution.py:218
  168.4 1.3 copy-done
  169.7 4.8 %all-to-all-done.3 = bf16[16,64,1024]{2,1,0:T(8,128)(2,1)} async-done(((bf16[16,64,1024]{2,1,0:T(8,128)(2,1)}), bf16[16,64,1024]{2,1,0:T(8,128)(2,1)}, u32[]{:S(2)}, u32[]{:S(2)}) %all-to-all-start.3) | async-done | bytes 2097184 | tf_op jit(solution)/shard_map/all_to_all | solution.py:300
  174.5 15.6 %all-to-all-start.2 = ((bf16[32,128,256]{2,1,0:T(8,128)(2,1)}), bf16[32,128,256]{2,1,0:T(8,128)(2,1)S(1)}, u32[]{:S(2)}, u32[]{:S(2)}) async-start(bf16[32,128,256]{2,1,0:T(8,128)(2,1)} %bitcast.83), calls=%async_computation.3 | async-start | bytes 4194304 | tf_op jit(solution)/shard_map/all_to_all | solution.py:300
  190.1 2.0 convert_reduce_fusion
  192.9 0.7 dynamic-slice_bitcast_fusion
  193.6 6.0 %collective-permute-start.10 = (bf16[128,512]{1,0:T(8,128)(2,1)}, bf16[128,512]{1,0:T(8,128)(2,1)S(1)}, u32[]{:S(2)}, u32[]{:S(2)}) collective-permute-start(bf16[128,512]{1,0:T(8,128)(2,1)} %get-tuple-element.39), channel_id=1, source_target_pairs={{0,2},{1,3},{2,0},{3,1},{4,6},{5,7},{6,4},{7,5},{8,10},{9,11},{10,... | collective-permute-start | bytes 393224 | tf_op jit(solution)/shard_map/ppermute | solution.py:305
  199.6 6.5 %collective-permute-start.11 = (bf16[128,512]{1,0:T(8,128)(2,1)S(1)}, bf16[128,512]{1,0:T(8,128)(2,1)S(1)}, u32[]{:S(2)}, u32[]{:S(2)}) collective-permute-start(bf16[128,512]{1,0:T(8,128)(2,1)S(1)} %get-tuple-element.38), channel_id=1, source_target_pairs={{0,3},{1,0},{2,1},{3,2},{4,7},{5,4},{6,5},{7,6},{8,11},{9,8},{10,9... | collective-permute-start | bytes 393224 | tf_op jit(solution)/shard_map/ppermute | solution.py:305
  206.1 0.9 collective-permute-start.9
  207.1 14.2 %collective-permute-done.10.refs_2_ = bf16[128,512]{1,0:T(8,128)(2,1)S(1)} collective-permute-done((bf16[128,512]{1,0:T(8,128)(2,1)}, bf16[128,512]{1,0:T(8,128)(2,1)S(1)}, u32[]{:S(2)}, u32[]{:S(2)}) %collective-permute-start.10) | collective-permute-done | bytes 131104 | tf_op jit(solution)/shard_map/ppermute | solution.py:305
  221.3 3.8 %collective-permute-done.9.refs_1_ = bf16[128,512]{1,0:T(8,128)(2,1)S(1)} collective-permute-done((bf16[128,512]{1,0:T(8,128)(2,1)S(1)}, bf16[128,512]{1,0:T(8,128)(2,1)S(1)}, u32[]{:S(2)}, u32[]{:S(2)}) %collective-permute-start.9) | collective-permute-done | bytes 131104 | tf_op jit(solution)/shard_map/ppermute | solution.py:305
  225.1 1.6 gather_gradients.1
  226.7 2.3 copy.22
  228.9 0.7 copy.36
  (38 shorter events, 1.3 us)
Async XLA Ops:
  7.2 102.2 %all-gather.2.cloned.1.call-start = ((), (), s32[]{:S(2)}) async-start(), calls=%async_computation.6 | async-start | bytes 5242880 | tf_op jit(solution)/shard_map/all_gather | solution.py:361
  7.9 23.0 %collective-permute-start = (bf16[64,1024]{1,0:T(8,128)(2,1)}, bf16[64,1024]{1,0:T(8,128)(2,1)S(1)}, u32[]{:S(2)}, u32[]{:S(2)}) collective-permute-start(bf16[64,1024]{1,0:T(8,128)(2,1)} %param.10), channel_id=1, source_target_pairs={{0,0},{1,64},{2,32},{3,96},{4,4},{5,68},{6,36},{7,100},{8,8},{9,72... | collective-permute-start | bytes 393224 | tf_op jit(solution)/shard_map/ppermute | solution.py:329
  9.5 21.6 %collective-permute-start.1 = (bf16[64,1024]{1,0:T(8,128)(2,1)}, bf16[64,1024]{1,0:T(8,128)(2,1)S(1)}, u32[]{:S(2)}, u32[]{:S(2)}) collective-permute-start(bf16[64,1024]{1,0:T(8,128)(2,1)} %param.10), channel_id=1, source_target_pairs={{0,4},{1,68},{2,36},{3,100},{4,8},{5,72},{6,40},{7,104},{8,12},{9,... | collective-permute-start | bytes 393224 | tf_op jit(solution)/shard_map/ppermute | solution.py:329
  11.1 19.9 %collective-permute-start.2 = (bf16[64,1024]{1,0:T(8,128)(2,1)}, bf16[64,1024]{1,0:T(8,128)(2,1)S(1)}, u32[]{:S(2)}, u32[]{:S(2)}) collective-permute-start(bf16[64,1024]{1,0:T(8,128)(2,1)} %param.10), channel_id=1, source_target_pairs={{0,8},{1,72},{2,40},{3,104},{4,12},{5,76},{6,44},{7,108},{8,0},{9,... | collective-permute-start | bytes 393224 | tf_op jit(solution)/shard_map/ppermute | solution.py:329
  14.0 17.1 %collective-permute-start.3 = (bf16[64,1024]{1,0:T(8,128)(2,1)}, bf16[64,1024]{1,0:T(8,128)(2,1)S(1)}, u32[]{:S(2)}, u32[]{:S(2)}) collective-permute-start(bf16[64,1024]{1,0:T(8,128)(2,1)} %param.10), channel_id=1, source_target_pairs={{0,12},{1,76},{2,44},{3,108},{4,0},{5,64},{6,32},{7,96},{8,4},{9,6... | collective-permute-start | bytes 393224 | tf_op jit(solution)/shard_map/ppermute | solution.py:329
  17.5 34.1 %all-to-all-start = ((bf16[4,128,768]{2,1,0:T(8,128)(2,1)}), bf16[4,128,768]{2,1,0:T(8,128)(2,1)S(1)}, u32[]{:S(2)}, u32[]{:S(2)}) async-start(bf16[4,128,768]{2,1,0:T(8,128)(2,1)} %pack_heads.1), calls=%async_computation | async-start | bytes 1572864 | tf_op jit(solution)/shard_map/all_to_all | solution.py:300
  31.1 25.7 %collective-permute-start.4 = (bf16[4,64,1024]{2,1,0:T(8,128)(2,1)S(1)}, bf16[4,64,1024]{2,1,0:T(8,128)(2,1)}, u32[]{:S(2)}, u32[]{:S(2)}) collective-permute-start(bf16[4,64,1024]{2,1,0:T(8,128)(2,1)S(1)} %bitcast_dynamic-update-slice_fusion.6), channel_id=1, source_target_pairs={{0,16},{16,64},{64,80},{80,0},{1,17},{17,65},{65,81},{81,1},{2,18}... | collective-permute-start | bytes 1572872 | tf_op jit(solution)/shard_map/ppermute | solution.py:305
  33.1 25.6 %collective-permute-start.5 = (bf16[4,64,1024]{2,1,0:T(8,128)(2,1)S(1)}, bf16[4,64,1024]{2,1,0:T(8,128)(2,1)S(1)}, u32[]{:S(2)}, u32[]{:S(2)}) collective-permute-start(bf16[4,64,1024]{2,1,0:T(8,128)(2,1)S(1)} %bitcast_dynamic-update-slice_fusion.6), channel_id=1, source_target_pairs={{0,64},{16,80},{64,0},{80,16},{1,65},{17,81},{65,1},{81,17},{2,66}... | collective-permute-start | bytes 1572872 | tf_op jit(solution)/shard_map/ppermute | solution.py:305
  34.0 25.5 %collective-permute-start.6 = (bf16[4,64,1024]{2,1,0:T(8,128)(2,1)S(1)}, bf16[4,64,1024]{2,1,0:T(8,128)(2,1)}, u32[]{:S(2)}, u32[]{:S(2)}) collective-permute-start(bf16[4,64,1024]{2,1,0:T(8,128)(2,1)S(1)} %bitcast_dynamic-update-slice_fusion.6), channel_id=1, source_target_pairs={{0,80},{16,0},{64,16},{80,64},{1,81},{17,1},{65,17},{81,65},{2,82}... | collective-permute-start | bytes 1572872 | tf_op jit(solution)/shard_map/ppermute | solution.py:305
  51.5 1.6 copy-start.4
  53.1 28.2 %all-to-all-start.1 = ((bf16[8,512,256]{2,1,0:T(8,128)(2,1)}), bf16[8,512,256]{2,1,0:T(8,128)(2,1)S(1)}, u32[]{:S(2)}, u32[]{:S(2)}) async-start(bf16[8,512,256]{2,1,0:T(8,128)(2,1)} %broadcast_in_dim.78), calls=%async_computation.1 | async-start | bytes 4194304 | tf_op jit(solution)/shard_map/all_to_all | solution.py:300
  56.7 169.9 %reduce-scatter.2.cloned.1.call-start = ((), (), s32[]{:S(2)}) async-start(), calls=%async_computation.5 | async-start | bytes 5242880 | tf_op jit(solution)/shard_map/reduce_scatter | solution.py:395
  61.4 37.9 %collective-permute-start.7 = (bf16[4,4,64,1024]{3,2,1,0:T(8,128)(2,1)}, bf16[4,4,64,1024]{3,2,1,0:T(8,128)(2,1)}, u32[]{:S(2)}, u32[]{:S(2)}) collective-permute-start(bf16[4,4,64,1024]{3,2,1,0:T(8,128)(2,1)} %bitcast_dynamic-update-slice_fusion.2), channel_id=1, source_target_pairs={{0,32},{32,0},{1,33},{33,1},{2,34},{34,2},{3,35},{35,3},{4,36},{36... | collective-permute-start | bytes 6291464 | tf_op jit(solution)/shard_map/ppermute | solution.py:305
  81.4 17.9 %copy-start.1 = (bf16[8,512,256]{2,1,0:T(8,128)(2,1)}, bf16[8,512,256]{2,1,0:T(8,128)(2,1)S(1)}, u32[]{:S(2)}) copy-start(bf16[8,512,256]{2,1,0:T(8,128)(2,1)S(1)} %all-to-all-done.1) | copy-start | bytes 6291460
  99.3 3.4 %copy-start.2 = (bf16[512,512]{1,0:T(8,128)(2,1)}, bf16[512,512]{1,0:T(8,128)(2,1)S(1)}, u32[]{:S(2)}) copy-start(bf16[512,512]{1,0:T(8,128)(2,1)S(1)} %get-tuple-element.15.att_t_ref) | copy-start | bytes 1572868
  109.3 1.0 copy-start.3
  110.3 7.6 %copy-start.5 = (bf16[4,512,1024]{2,1,0:T(8,128)(2,1)S(1)}, bf16[4,512,1024]{2,1,0:T(8,128)(2,1)}, u32[]{:S(2)}) copy-start(bf16[4,512,1024]{2,1,0:T(8,128)(2,1)} %all-gather.2.cloned.1.call-done) | copy-start | bytes 12582916
  113.4 4.6 %collective-permute-start.8 = (bf16[2,512,1024]{2,1,0:T(8,128)(2,1)S(1)}, bf16[2,512,1024]{2,1,0:T(8,128)(2,1)S(1)}, u32[]{:S(2)}, u32[]{:S(2)}) collective-permute-start(bf16[2,512,1024]{2,1,0:T(8,128)(2,1)S(1)} %convert_bitcast_fusion.1), channel_id=1, source_target_pairs={{0,32},{32,0},{1,33},{33,1},{2,34},{34,2},{3,35},{35,3},{4,36},{36... | collective-permute-start | bytes 6291464 | tf_op jit(solution)/shard_map/ppermute | solution.py:305
  120.6 53.9 %all-to-all-start.3 = ((bf16[16,64,1024]{2,1,0:T(8,128)(2,1)}), bf16[16,64,1024]{2,1,0:T(8,128)(2,1)}, u32[]{:S(2)}, u32[]{:S(2)}) async-start(bf16[16,64,1024]{2,1,0:T(8,128)(2,1)} %bitcast.89), calls=%async_computation.4 | async-start | bytes 4194304 | tf_op jit(solution)/shard_map/all_to_all | solution.py:300
  168.4 1.3 copy-start
  174.5 50.6 %all-to-all-start.2 = ((bf16[32,128,256]{2,1,0:T(8,128)(2,1)}), bf16[32,128,256]{2,1,0:T(8,128)(2,1)S(1)}, u32[]{:S(2)}, u32[]{:S(2)}) async-start(bf16[32,128,256]{2,1,0:T(8,128)(2,1)} %bitcast.83), calls=%async_computation.3 | async-start | bytes 4194304 | tf_op jit(solution)/shard_map/all_to_all | solution.py:300
  192.1 34.5 %collective-permute-start.12 = (f32[64,1024]{1,0:T(8,128)S(1)}, f32[64,1024]{1,0:T(8,128)S(1)}, u32[]{:S(2)}, u32[]{:S(2)}) collective-permute-start(f32[64,1024]{1,0:T(8,128)S(1)} %convert_reduce_fusion), channel_id=1, source_target_pairs={{0,0},{64,1},{32,2},{96,3},{4,4},{68,5},{36,6},{100,7},{8,8},{72,9... | collective-permute-start | bytes 786440 | tf_op jit(solution)/shard_map/ppermute | solution.py:333
  193.6 27.7 %collective-permute-start.10 = (bf16[128,512]{1,0:T(8,128)(2,1)}, bf16[128,512]{1,0:T(8,128)(2,1)S(1)}, u32[]{:S(2)}, u32[]{:S(2)}) collective-permute-start(bf16[128,512]{1,0:T(8,128)(2,1)} %get-tuple-element.39), channel_id=1, source_target_pairs={{0,2},{1,3},{2,0},{3,1},{4,6},{5,7},{6,4},{7,5},{8,10},{9,11},{10,... | collective-permute-start | bytes 393224 | tf_op jit(solution)/shard_map/ppermute | solution.py:305
  199.6 21.7 %collective-permute-start.11 = (bf16[128,512]{1,0:T(8,128)(2,1)S(1)}, bf16[128,512]{1,0:T(8,128)(2,1)S(1)}, u32[]{:S(2)}, u32[]{:S(2)}) collective-permute-start(bf16[128,512]{1,0:T(8,128)(2,1)S(1)} %get-tuple-element.38), channel_id=1, source_target_pairs={{0,3},{1,0},{2,1},{3,2},{4,7},{5,4},{6,5},{7,6},{8,11},{9,8},{10,9... | collective-permute-start | bytes 393224 | tf_op jit(solution)/shard_map/ppermute | solution.py:305
  206.1 19.0 %collective-permute-start.9 = (bf16[128,512]{1,0:T(8,128)(2,1)S(1)}, bf16[128,512]{1,0:T(8,128)(2,1)S(1)}, u32[]{:S(2)}, u32[]{:S(2)}) collective-permute-start(bf16[128,512]{1,0:T(8,128)(2,1)S(1)} %get-tuple-element.40), channel_id=1, source_target_pairs={{0,1},{1,2},{2,3},{3,0},{4,5},{5,6},{6,7},{7,4},{8,9},{9,10},{10,1... | collective-permute-start | bytes 393224 | tf_op jit(solution)/shard_map/ppermute | solution.py:305
Sparse Core Ops, SparseCore 0:
  9.7 63.3 all-gather.1
  109.4 65.6 reduce-scatter.1
